TPU v7x, 512 devices: a whole 4x8x8 slice. The times are simulated.
512 devices in a mesh: layer: 8 (over z), row: 64 (over x, y, core).
Axes of the slice: x: 4, y: 8, z: 8, core: 2. Of those that a mesh axis runs over, the one named last changes fastest.
Arguments:
- leaf_rhs: float32 [8, 64, 256, 384], P('layer', 'row'), may hold values from -6 to 6
- leaf_inverse: float32 [8, 64, 256, 256], P('layer', 'row'), may hold values from -0.375 to 0.375
- leaf_coupling: float32 [8, 64, 4, 512, 256], P('layer', 'row'), may hold values from -0.046875 to 0.046875
- parent: int32 [8, 64], P('layer', 'row'), may hold values from 0 to 3
- sep_rhs: float32 [8, 4, 512, 384], P('layer', None, 'row'), may hold values from -6 to 6
- sep_inverse: float32 [8, 4, 512, 512], P('layer', None, 'row'), may hold values from -0.25 to 0.25
- sep_coupling: float32 [8, 3, 512, 512], P('layer', None, 'row'), may hold values from -0.125 to 0.125
- root_coupling: float32 [8, 512, 512], P('layer', 'row'), may hold values from -0.09375 to 0.09375
- root_rhs: float32 [512, 384], P('row'), may hold values from -6 to 6
- root_inverse: float32 [512, 512], P('row'), may hold values from -0.25 to 0.25
Outputs:
- sep_solution: float32 [8, 4, 512, 384], P('layer', None, 'row')
- root_solution: float32 [512, 384], P('row')
All inputs are finite; a program needn't handle non-finite values.
Results may differ from a plain program's by a relative error of at most 0.0003.
Values sent between devices are 32-bit elements; how exact they have to be, the bound alone decides.
No kernel may reach another device: no remote copies, remote signals or barrier semaphores. Data moves between devices by JAX's collectives and lax.ppermute only.
A program may use at most 64 MiB of HBM per device.

v0:
```python
import jax
import jax.numpy as jnp
from jax import lax
from jax.sharding import PartitionSpec as P


def body(
    leaf_rhs,
    leaf_inverse,
    leaf_coupling,
    parent,
    sep_rhs,
    sep_inverse,
    sep_coupling,
    root_coupling,
    root_rhs,
    root_inverse,
):
    highest = lax.Precision.HIGHEST
    sep_count = sep_rhs.shape[1]
    row_count = sep_rhs.shape[2]
    row_start = lax.axis_index("row") * row_count
    leaf_solution = jnp.dot(leaf_inverse[0, 0], leaf_rhs[0, 0], precision=highest)
    levels = jnp.arange(sep_count, dtype=jnp.int32)
    keep_mask = (levels >= parent[0, 0]).astype(jnp.float32)
    coupled = (
        jnp.einsum("kwb,bc->kwc", leaf_coupling[0, 0], leaf_solution, precision=highest)
        * keep_mask[:, None, None]
    )
    own_rhs = lax.dynamic_update_slice_in_dim(jnp.zeros_like(coupled), sep_rhs[0], row_start, 1)
    residual = lax.psum(own_rhs - coupled, "row")
    residual_list = [residual[k] for k in range(sep_count)]
    local_rows = [
        jnp.dot(sep_inverse[0, k], residual_list[k], precision=highest) for k in range(sep_count)
    ]
    solved = []
    gathered = None
    for k in range(sep_count):
        current = local_rows[k]
        if k > 0:
            current = current - jnp.dot(sep_coupling[0, k - 1], gathered, precision=highest)
        solved.append(current)
        gathered = lax.all_gather(current, "row", axis=0, tiled=True)
    sep_out = jnp.stack(solved)[None]
    root_term = jnp.dot(root_coupling[0], gathered, precision=highest)
    root_sum = lax.psum(root_term, "layer")
    root_residual = root_rhs - root_sum
    root_out = jnp.dot(
        root_inverse, lax.all_gather(root_residual, "row", axis=0, tiled=True), precision=highest
    )
    return (sep_out, root_out)


def solution(mesh):
    return jax.shard_map(
        body,
        mesh=mesh,
        in_specs=(
            P("layer", "row", None, None),
            P("layer", "row", None, None),
            P("layer", "row", None, None, None),
            P("layer", "row"),
            P("layer", None, "row", None),
            P("layer", None, "row", None),
            P("layer", None, "row", None),
            P("layer", "row", None),
            P("row", None),
            P("row", None),
        ),
        out_specs=(P("layer", None, "row", None), P("row", None)),
        check_vma=False,
    )
```

profile of v0, /device:TPU:1, one launch (start us, length us, event | category | flops | bytes accessed | tf_op | source)
XLA Modules:
  0.0 522.9 jit_solution(4747656309365464238)
XLA Ops:
  7.2 0.0 copy-start
  7.2 0.0 all-reduce.2.cloned.1.call-start
  7.2 1.2 copy.12
  9.1 1.9 convolution_bitcast_fusion
  11.0 2.1 broadcast_in_dim.7
  13.1 4.4 dynamic_update_slice.3
  17.5 0.0 copy-done
  17.5 5.6 %bitcast_subtract_fusion = f32[4,512,384]{1,2,0:T(8,128)} fusion(f32[4,512,384]{1,2,0:T(8,128)} %dynamic_update_slice.3, f32[256,384,1]{0,1,2:T(8,128)S(1)} %convolution_bitcast_fusion, f32[1,1,4,512,256]{4,3,2,1,0:T(8,128)S(1)} %copy-done, f32[4]{0:T(128)S(1)} %compare_convert_fusion), kind=kOutput, calls=%fused_computation | convolution fusion | flops 2417491968 | bytes 8781840 | tf_op jit(solution)/shard_map/kwb,bc->kwc/dot_general | solution.py:27
  23.1 0.0 all-reduce.2.cloned.1.call-update
  23.2 207.1 %all-reduce.2.cloned.1.call-done = f32[4,512,384]{1,2,0:T(8,128)} async-done(((f32[4,512,384]{1,2,0:T(8,128)}), f32[4,512,384]{1,2,0:T(8,128)}) %all-reduce.2.cloned.1.call-update) | async-done | bytes 3145744 | tf_op jit(solution)/shard_map/psum | solution.py:31
  230.2 0.0 copy-done.2
  230.2 2.0 fusion.7
  232.2 50.8 %all_gather.15 = f32[512,384]{1,0:T(8,128)S(1)} all-gather(f32[8,384]{1,0:T(8,128)S(1)} %bitcast.80), channel_id=1, replica_groups=mesh['layer'=8,'row'=64] {'row'}, dimensions={0}, use_global_device_ids=true | all-gather | bytes 798720 | tf_op jit(solution)/shard_map/all_gather | solution.py:43
  283.0 1.8 fusion.6
  284.9 0.0 copy-done.3
  284.9 0.0 copy-start.4
  284.9 0.5 convolution_subtract_fusion.2
  285.4 48.8 %all_gather.16 = f32[512,384]{1,0:T(8,128)S(1)} all-gather(f32[8,384]{1,0:T(8,128)S(1)} %bitcast.82), channel_id=1, replica_groups=mesh['layer'=8,'row'=64] {'row'}, dimensions={0}, use_global_device_ids=true | all-gather | bytes 798720 | tf_op jit(solution)/shard_map/all_gather | solution.py:43
  334.2 0.0 copy-done.1
  334.2 0.0 copy-start.5
  334.2 0.7 fusion.5
  334.9 0.5 convolution_subtract_fusion.1
  335.5 48.9 %all_gather.17 = f32[512,384]{1,0:T(8,128)S(1)} all-gather(f32[8,384]{1,0:T(8,128)S(1)} %bitcast.84), channel_id=1, replica_groups=mesh['layer'=8,'row'=64] {'row'}, dimensions={0}, use_global_device_ids=true | all-gather | bytes 798720 | tf_op jit(solution)/shard_map/all_gather | solution.py:43
  384.3 0.7 fusion.4
  385.1 0.5 convolution_subtract_fusion
  385.6 48.7 %all_gather.18 = f32[512,384]{1,0:T(8,128)S(1)} all-gather(f32[8,384]{1,0:T(8,128)S(1)} %bitcast.86), channel_id=1, replica_groups=mesh['layer'=8,'row'=64] {'row'}, dimensions={0}, use_global_device_ids=true | all-gather | bytes 798720 | tf_op jit(solution)/shard_map/all_gather | solution.py:43
  434.3 0.0 copy-done.4
  434.3 0.5 convolution_bitcast_fusion.2
  434.8 23.6 %psum.15 = f32[8,384]{1,0:T(8,128)S(1)} all-reduce(f32[8,384]{1,0:T(8,128)S(1)} %convolution_bitcast_fusion.2), channel_id=1, replica_groups=mesh['layer'=8,'row'=64] {'layer'}, use_global_device_ids=true, to_apply=%region_1.0 | all-reduce | flops 3072 | bytes 24576 | tf_op jit(solution)/shard_map/psum | solution.py:46
  458.4 55.9 %all_gather.19 = f32[512,384]{1,0:T(8,128)S(1)} all-gather(f32[8,384]{1,0:T(8,128)S(1)} %sub.31), channel_id=1, replica_groups=mesh['layer'=8,'row'=64] {'row'}, dimensions={0}, use_global_device_ids=true | all-gather | bytes 798720 | tf_op jit(solution)/shard_map/all_gather | solution.py:49
  514.3 1.1 convolution_bitcast_fusion.1
  515.4 0.6 maximum_bitcast_fusion
  (8 shorter events, 0.0 us)
Async XLA Ops:
  7.2 10.3 %copy-start = (f32[1,1,4,512,256]{4,3,2,1,0:T(8,128)S(1)}, f32[1,1,4,512,256]{4,3,2,1,0:T(8,128)}, u32[]{:S(2)}) copy-start(f32[1,1,4,512,256]{4,3,2,1,0:T(8,128)} %param.12) | copy-start | bytes 6291460
  7.2 223.1 %all-reduce.2.cloned.1.call-start = ((), (), s32[]{:S(2)}) async-start(), calls=%async_computation | async-start | bytes 6291456 | tf_op jit(solution)/shard_map/psum | solution.py:31
  23.1 207.1 %copy-start.2 = (f32[1,4,8,512]{3,2,1,0:T(8,128)S(1)}, f32[1,4,8,512]{3,2,1,0:T(8,128)}, u32[]{:S(2)}) copy-start(f32[1,4,8,512]{3,2,1,0:T(8,128)} %param.15) | copy-start | bytes 196612
  23.1 261.7 %copy-start.3 = (f32[1,3,8,512]{3,2,1,0:T(8,128)S(1)}, f32[1,3,8,512]{3,2,1,0:T(8,128)}, u32[]{:S(2)}) copy-start(f32[1,3,8,512]{3,2,1,0:T(8,128)} %param.16) | copy-start | bytes 147460
  230.2 104.0 %copy-start.1 = (f32[4,512,384]{1,2,0:T(8,128)S(1)}, f32[4,512,384]{1,2,0:T(8,128)}, u32[]{:S(2)}) copy-start(f32[4,512,384]{1,2,0:T(8,128)} %all-reduce.2.cloned.1.call-done) | copy-start | bytes 9437188
  284.9 149.4 %copy-start.4 = (f32[1,8,512]{2,1,0:T(8,128)S(1)}, f32[1,8,512]{2,1,0:T(8,128)}, u32[]{:S(2)}) copy-start(f32[1,8,512]{2,1,0:T(8,128)} %param.17) | copy-start | bytes 49156
  285.4 173.0 %copy-start.6 = (f32[8,384]{1,0:T(8,128)S(1)}, f32[8,384]{1,0:T(8,128)}, u32[]{:S(2)}) copy-start(f32[8,384]{1,0:T(8,128)} %param.18) | copy-start | bytes 36868
  334.2 180.1 %copy-start.5 = (f32[8,512]{1,0:T(8,128)S(1)}, f32[8,512]{1,0:T(8,128)}, u32[]{:S(2)}) copy-start(f32[8,512]{1,0:T(8,128)} %param.19) | copy-start | bytes 49156
Sparse Core Ops, SparseCore 0:
  23.3 206.9 all-reduce.1
where the time goes:
time: 523 us
  blocking collectives  277 us (53%)
  waiting for transfers between devices  207 us (40%)
  matrix products  16 us (3%)
  between operations  14.8 us (3%)
  local copies, waits for them, and re-layouts  7.74 us (1%)
    psum x1, waiting for transfers between devices, body(): residual = lax.psum(own_rhs - coupled, 'row')  207 us
    all_gather x4, blocking collectives, body(): gathered = lax.all_gather(current, 'row', axis=0, tiled=True)  197 us
    all_gather x1, blocking collectives, body(): lax.all_gather(root_residual, 'row', axis=0, tiled=True)  55.9 us
    psum x1, blocking collectives, body(): root_sum = lax.psum(root_term, 'layer')  23.6 us
  transfers between devices with their start and end apart: 1, of which 1 were waited for; matrix products, arithmetic and copies ran while one was open for 0% of the time, Pallas kernels for 0%

commit v1 on v0

--- a/solution.py
+++ b/solution.py
@@ -46,7 +46,11 @@
     root_sum = lax.psum(root_term, "layer")
     root_residual = root_rhs - root_sum
     root_out = jnp.dot(
-        root_inverse, lax.all_gather(root_residual, "row", axis=0, tiled=True), precision=highest
+        root_inverse,
+        jnp.concatenate(
+            lax.all_to_all(jnp.stack([root_residual] * lax.axis_size("row")), "row", 0, 0), axis=0
+        ),
+        precision=highest,
     )
     return (sep_out, root_out)
 

time: 523 us -> 506 us (0.967)
  blocking collectives: 277 us -> 221 us
  waiting for transfers between devices: 207 us -> 230 us
  starting transfers between devices: 0.04 us -> 14.9 us
    all_gather x1 -> x0, blocking collectives: 55.9 us -> none  [body(): lax.all_gather(root_residual, 'row', axis=0, tiled=True)]
    all_to_all x0 -> x1, waiting for transfers between devices: none -> 22.4 us  [body(): lax.all_to_all(jnp.stack([root_residual] * lax.axis_size('row')), 'row',...]
    all_to_all x0 -> x1, starting transfers between devices: none -> 14.8 us  [body(): lax.all_to_all(jnp.stack([root_residual] * lax.axis_size('row')), 'row',...]
  transfers between devices with their start and end apart: 1 -> 2, of which waited for: 1 -> 2; matrix products, arithmetic and copies ran while one was open for 0% -> 0% of each run, Pallas kernels for 0% -> 0%
where the time goes in v1:
time: 506 us; the launch traced here: 505 us
  waiting for transfers between devices  230 us (45%)
  blocking collectives  221 us (44%)
  matrix products  16 us (3%)
  starting transfers between devices  14.9 us (3%)
  between operations  14.8 us (3%)
  local copies, waits for them, and re-layouts  8.69 us (2%)
    psum x1, waiting for transfers between devices, body(): residual = lax.psum(own_rhs - coupled, 'row')  207 us
    all_gather x4, blocking collectives, body(): gathered = lax.all_gather(current, 'row', axis=0, tiled=True)  197 us
    psum x1, blocking collectives, body(): root_sum = lax.psum(root_term, 'layer')  23.6 us
    all_to_all x1, waiting for transfers between devices, body(): lax.all_to_all(jnp.stack([root_residual] * lax.axis_size('row')), 'row',...  22.4 us
    all_to_all x1, starting transfers between devices, body(): lax.all_to_all(jnp.stack([root_residual] * lax.axis_size('row')), 'row',...  14.8 us
  transfers between devices with their start and end apart: 2, of which 2 were waited for; matrix products, arithmetic and copies ran while one was open for 0% of the time, Pallas kernels for 0%

profile of v1, /device:TPU:1, one launch (start us, length us, event | category | flops | bytes accessed | tf_op | source)
XLA Modules:
  0.0 505.3 jit_solution(14717193746604218605)
XLA Ops:
  7.2 0.0 copy-start
  7.2 0.0 all-reduce.2.cloned.1.call-start
  7.2 1.2 copy.12
  9.1 1.9 convolution_bitcast_fusion
  11.0 2.1 broadcast_in_dim.7
  13.1 4.4 dynamic_update_slice.3
  17.5 0.0 copy-done
  17.5 5.6 %bitcast_subtract_fusion = f32[4,512,384]{1,2,0:T(8,128)} fusion(f32[4,512,384]{1,2,0:T(8,128)} %dynamic_update_slice.3, f32[256,384,1]{0,1,2:T(8,128)S(1)} %convolution_bitcast_fusion, f32[1,1,4,512,256]{4,3,2,1,0:T(8,128)S(1)} %copy-done, f32[4]{0:T(128)S(1)} %compare_convert_fusion), kind=kOutput, calls=%fused_computation | convolution fusion | flops 2417491968 | bytes 8781840 | tf_op jit(solution)/shard_map/kwb,bc->kwc/dot_general | solution.py:27
  23.1 0.0 all-reduce.2.cloned.1.call-update
  23.2 207.1 %all-reduce.2.cloned.1.call-done = f32[4,512,384]{1,2,0:T(8,128)} async-done(((f32[4,512,384]{1,2,0:T(8,128)}), f32[4,512,384]{1,2,0:T(8,128)}) %all-reduce.2.cloned.1.call-update) | async-done | bytes 3145744 | tf_op jit(solution)/shard_map/psum | solution.py:31
  230.3 0.0 copy-done.2
  230.3 2.0 fusion.7
  232.3 50.8 %all_gather.12 = f32[512,384]{1,0:T(8,128)S(1)} all-gather(f32[8,384]{1,0:T(8,128)S(1)} %bitcast.82), channel_id=1, replica_groups=mesh['layer'=8,'row'=64] {'row'}, dimensions={0}, use_global_device_ids=true | all-gather | bytes 798720 | tf_op jit(solution)/shard_map/all_gather | solution.py:43
  283.1 1.8 fusion.6
  284.9 0.0 copy-done.3
  285.0 0.0 copy-start.4
  285.0 0.5 convolution_subtract_fusion.2
  285.5 48.8 %all_gather.13 = f32[512,384]{1,0:T(8,128)S(1)} all-gather(f32[8,384]{1,0:T(8,128)S(1)} %bitcast.84), channel_id=1, replica_groups=mesh['layer'=8,'row'=64] {'row'}, dimensions={0}, use_global_device_ids=true | all-gather | bytes 798720 | tf_op jit(solution)/shard_map/all_gather | solution.py:43
  334.3 0.0 copy-done.1
  334.3 0.7 fusion.5
  335.0 0.5 convolution_subtract_fusion.1
  335.6 48.9 %all_gather.14 = f32[512,384]{1,0:T(8,128)S(1)} all-gather(f32[8,384]{1,0:T(8,128)S(1)} %bitcast.86), channel_id=1, replica_groups=mesh['layer'=8,'row'=64] {'row'}, dimensions={0}, use_global_device_ids=true | all-gather | bytes 798720 | tf_op jit(solution)/shard_map/all_gather | solution.py:43
  384.4 0.7 fusion.4
  385.1 0.5 convolution_subtract_fusion
  385.7 48.8 %all_gather.15 = f32[512,384]{1,0:T(8,128)S(1)} all-gather(f32[8,384]{1,0:T(8,128)S(1)} %bitcast.88), channel_id=1, replica_groups=mesh['layer'=8,'row'=64] {'row'}, dimensions={0}, use_global_device_ids=true | all-gather | bytes 798720 | tf_op jit(solution)/shard_map/all_gather | solution.py:43
  434.4 0.5 convolution_bitcast_fusion.2
  434.9 23.6 %psum.15 = f32[8,384]{1,0:T(8,128)S(1)} all-reduce(f32[8,384]{1,0:T(8,128)S(1)} %convolution_bitcast_fusion.2), channel_id=1, replica_groups=mesh['layer'=8,'row'=64] {'layer'}, use_global_device_ids=true, to_apply=%region_1.0 | all-reduce | flops 3072 | bytes 24576 | tf_op jit(solution)/shard_map/psum | solution.py:46
  458.6 0.9 stack.17
  459.5 14.8 %all-to-all-start = ((f32[64,8,384]{2,1,0:T(8,128)}), f32[64,8,384]{2,1,0:T(8,128)S(1)}, u32[]{:S(2)}, u32[]{:S(2)}) async-start(f32[64,8,384]{2,1,0:T(8,128)} %stack.17), calls=%async_computation | async-start | bytes 1572864 | tf_op jit(solution)/shard_map/all_to_all | solution.py:51
  474.3 0.6 maximum_bitcast_fusion
  475.0 22.4 %all-to-all-done = f32[64,8,384]{2,1,0:T(8,128)S(1)} async-done(((f32[64,8,384]{2,1,0:T(8,128)}), f32[64,8,384]{2,1,0:T(8,128)S(1)}, u32[]{:S(2)}, u32[]{:S(2)}) %all-to-all-start) | async-done | bytes 786464 | tf_op jit(solution)/shard_map/all_to_all | solution.py:51
  497.3 1.1 convolution_bitcast_fusion.1
  (10 shorter events, 0.0 us)
Async XLA Ops:
  7.2 10.3 %copy-start = (f32[1,1,4,512,256]{4,3,2,1,0:T(8,128)S(1)}, f32[1,1,4,512,256]{4,3,2,1,0:T(8,128)}, u32[]{:S(2)}) copy-start(f32[1,1,4,512,256]{4,3,2,1,0:T(8,128)} %param.12) | copy-start | bytes 6291460
  7.2 223.1 %all-reduce.2.cloned.1.call-start = ((), (), s32[]{:S(2)}) async-start(), calls=%async_computation.1 | async-start | bytes 6291456 | tf_op jit(solution)/shard_map/psum | solution.py:31
  23.1 207.2 %copy-start.2 = (f32[1,4,8,512]{3,2,1,0:T(8,128)S(1)}, f32[1,4,8,512]{3,2,1,0:T(8,128)}, u32[]{:S(2)}) copy-start(f32[1,4,8,512]{3,2,1,0:T(8,128)} %param.15) | copy-start | bytes 196612
  23.1 261.8 %copy-start.3 = (f32[1,3,8,512]{3,2,1,0:T(8,128)S(1)}, f32[1,3,8,512]{3,2,1,0:T(8,128)}, u32[]{:S(2)}) copy-start(f32[1,3,8,512]{3,2,1,0:T(8,128)} %param.16) | copy-start | bytes 147460
  230.3 104.0 %copy-start.1 = (f32[4,512,384]{1,2,0:T(8,128)S(1)}, f32[4,512,384]{1,2,0:T(8,128)}, u32[]{:S(2)}) copy-start(f32[4,512,384]{1,2,0:T(8,128)} %all-reduce.2.cloned.1.call-done) | copy-start | bytes 9437188
  285.0 149.4 %copy-start.4 = (f32[1,8,512]{2,1,0:T(8,128)S(1)}, f32[1,8,512]{2,1,0:T(8,128)}, u32[]{:S(2)}) copy-start(f32[1,8,512]{2,1,0:T(8,128)} %param.17) | copy-start | bytes 49156
  285.5 173.1 %copy-start.6 = (f32[8,384]{1,0:T(8,128)S(1)}, f32[8,384]{1,0:T(8,128)}, u32[]{:S(2)}) copy-start(f32[8,384]{1,0:T(8,128)} %param.18) | copy-start | bytes 36868
  335.6 161.8 %copy-start.5 = (f32[8,512]{1,0:T(8,128)S(1)}, f32[8,512]{1,0:T(8,128)}, u32[]{:S(2)}) copy-start(f32[8,512]{1,0:T(8,128)} %param.19) | copy-start | bytes 49156
  459.5 37.8 %all-to-all-start = ((f32[64,8,384]{2,1,0:T(8,128)}), f32[64,8,384]{2,1,0:T(8,128)S(1)}, u32[]{:S(2)}, u32[]{:S(2)}) async-start(f32[64,8,384]{2,1,0:T(8,128)} %stack.17), calls=%async_computation | async-start | bytes 1572864 | tf_op jit(solution)/shard_map/all_to_all | solution.py:51
Sparse Core Ops, SparseCore 0:
  23.3 206.9 all-reduce.1
